TPU v7x, 128 devices: a whole 4x4x4 slice. The times are simulated.
128 devices in a mesh: tile: 32 (over y, x_lo, z), angle: 4 (over x_hi, core).
Axes of the slice: x: 4 (x_hi: 2, x_lo: 2; x = x_hi * 2 + x_lo), y: 4, z: 4, core: 2. Of those that a mesh axis runs over, the one named last changes fastest.
Arguments:
- volume: float32 [96, 1024, 256], P(None, 'tile'), may hold values from -6 to 6
- measured: float32 [2, 32, 512, 8192], P(None, 'angle', 'tile'), may hold values from -1536 to 1536
- blocks: float32 [2, 32, 96, 16, 96], P(None, 'angle', 'tile'), may hold values from 0.1 to 1
- ray_lists: int32 [2, 32, 96], P(None, 'angle', 'tile'), may hold values from 0 to 31, as said below
- counts: int32 [2, 32, 32], P(None, 'angle', 'tile'), may hold values from 1 to 3
Outputs:
- volume_final: float32 [96, 1024, 256], P(None, 'tile')
Inputs may be any that keep to these rules, and one draw needn't show every extreme that they name: `ray_lists`: entry 3 * t + k names the ray tile that entry k of volume tile t touches: entry 0 is t itself, every entry lies within one ray tile of t. Only the first counts entries of a tile's list are used.
All inputs are finite; a program needn't handle non-finite values.
Results may differ from a plain program's by a relative error of at most 0.0001.
Values sent between devices are 32-bit elements; how exact they have to be, the bound alone decides.
A program may use at most 192 MiB of HBM per device.

v0:
```python
import jax
import jax.numpy as jnp
from jax import lax
from jax.sharding import PartitionSpec as P

RELAX = 1.0
TV_WEIGHT = 0.05
TV_EPSILON = 0.01


def padded_2(cells, sides, width):
    for axis, dim in sides:
        count = lax.axis_size(axis)
        ends = count - 1
        head = lax.slice_in_dim(cells, 0, width, axis=dim)
        tail = lax.slice_in_dim(cells, cells.shape[dim] - width, cells.shape[dim], axis=dim)
        cells = jnp.concatenate(
            [
                lax.ppermute(tail, axis, [(i, (i + 1) % count) for i in range(ends)]),
                cells,
                lax.ppermute(head, axis, [((i + 1) % count, i) for i in range(ends)]),
            ],
            axis=dim,
        )
    return cells


def passed_along(value, axis, steps):
    count = lax.axis_size(axis)
    leading, last = (max(0, -steps), min(count, count - steps))
    return lax.ppermute(value, axis, [(source, source + steps) for source in range(leading, last)])


def direction_term(volume, axis_pos):
    extent = volume.shape[axis_pos]
    edge_layer = lax.slice_in_dim(volume, extent - 1, extent, axis=axis_pos)
    ahead_layers = jnp.concatenate(
        [lax.slice_in_dim(volume, 1, extent, axis=axis_pos), edge_layer], axis=axis_pos
    )
    difference = ahead_layers - volume
    fluxes = difference / jnp.sqrt(difference * difference + TV_EPSILON)
    behind = jnp.concatenate(
        [jnp.zeros_like(edge_layer), lax.slice_in_dim(fluxes, 0, extent - 1, axis=axis_pos)],
        axis=axis_pos,
    )
    return behind - fluxes


def cross_term(volume, tile_index, tile_count):
    padded = padded_2(volume, (("tile", 1),), 1)
    first_row = volume[:, :1]
    last_row = volume[:, -1:]
    left_rim = jnp.where(tile_index == 0, first_row, padded[:, :1])
    right_rim = jnp.where(tile_index == tile_count - 1, last_row, padded[:, -1:])
    extended = jnp.concatenate([left_rim, volume, right_rim], axis=1)
    difference = extended[:, 1:] - extended[:, :-1]
    fluxes = difference / jnp.sqrt(difference * difference + TV_EPSILON)
    return fluxes[:, :-1] - fluxes[:, 1:]


def back_project(combined, nearby_resid):
    update = jnp.einsum("aodz,oadc->zc", combined, nearby_resid, precision=lax.Precision.HIGHEST)
    column_sums = jnp.sum(combined, axis=(0, 1, 2))
    return (update, column_sums)


def sum_angles(update, column_sums):
    return lax.psum((update, column_sums), "angle")


def per_device(volume, measured, blocks, ray_lists, counts):
    slab_depth, tile_rows, tile_cols = volume.shape
    cell_count = tile_rows * tile_cols
    tile_index = lax.axis_index("tile")
    tile_count = lax.axis_size("tile")
    slot_count = blocks.shape[2]
    for subset in range(blocks.shape[0]):
        tile_cells = volume.reshape(slab_depth, cell_count)
        weights = blocks[subset]
        offsets = ray_lists[subset] - tile_index
        live_slots = jnp.arange(slot_count, dtype=jnp.int32)[None, :] < counts[subset]
        offset_masks = jnp.stack(
            [(live_slots & (offsets == offset)).astype(jnp.float32) for offset in (-1, 0, 1)],
            axis=1,
        )
        combined = jnp.einsum(
            "aok,akdz->aodz", offset_masks, weights, precision=lax.Precision.HIGHEST
        )
        partial_proj = jnp.einsum(
            "aodz,zc->oadc", combined, tile_cells, precision=lax.Precision.HIGHEST
        )
        partial_rows = jnp.transpose(jnp.sum(combined, axis=3), (1, 0, 2))
        from_left, rows_left = passed_along((partial_proj[2], partial_rows[2]), "tile", 1)
        from_right, rows_right = passed_along((partial_proj[0], partial_rows[0]), "tile", -1)
        forward = partial_proj[1] + from_left + from_right
        row_sums = partial_rows[1] + rows_left + rows_right
        residual = (measured[subset] - forward) / row_sums[:, :, None]
        nearby_resid = padded_2(residual[None], (("tile", 0),), 1)
        update, column_sums = back_project(combined, nearby_resid)
        update, column_sums = sum_angles(update, column_sums)
        tile_cells = tile_cells + RELAX * update / column_sums[:, None]
        volume = tile_cells.reshape(slab_depth, tile_rows, tile_cols)
        total_term = (
            direction_term(volume, 0)
            + cross_term(volume, tile_index, tile_count)
            + direction_term(volume, 2)
        )
        volume = volume - TV_WEIGHT * total_term
    return volume


def solution(mesh):
    return jax.shard_map(
        per_device,
        mesh=mesh,
        in_specs=(
            P(None, "tile", None),
            P(None, "angle", "tile", None),
            P(None, "angle", "tile", None, None),
            P(None, "angle", "tile"),
            P(None, "angle", "tile"),
        ),
        out_specs=P(None, "tile", None),
        check_vma=False,
    )
```

profile of v0, /device:TPU:1, one launch (start us, length us, event | category | flops | bytes accessed | tf_op | source)
XLA Modules:
  0.0 704.8 jit_solution(13757854989659117555)
XLA Ops:
  9.2 4.6 reshape.331
  14.4 11.9 %convolution_bitcast_fusion.1 = f32[3,8,16,8192]{3,2,0,1:T(8,128)S(1)} fusion(f32[96,8192,1,1]{1,0,2,3:T(8,128)} %reshape.331, f32[8,3,16,96]{3,1,2,0:T(4,128)S(1)} %get-tuple-element.49), kind=kOutput, calls=%fused_computation.7 | convolution fusion | flops 3623878656 | bytes 15876096 | tf_op jit(solution)/shard_map/aodz,zc->oadc/dot_general | solution.py:89
  28.9 6.3 collective-permute-start
  42.2 80.6 %collective-permute-done.2 = f32[8,16]{1,0:T(8,128)S(1)} collective-permute-done((f32[8,16]{1,0:T(8,128)S(1)}, f32[8,16]{1,0:T(8,128)S(1)}, u32[]{:S(2)}, u32[]{:S(2)}) %collective-permute-start.2) | collective-permute-done | bytes 544 | tf_op jit(solution)/shard_map/ppermute | solution.py:31
  122.8 5.8 collective-permute-done.3
  128.6 8.0 %fusion.19 = f32[1,8,16,8192]{3,2,1,0:T(8,128)} fusion(f32[8,16,8192]{2,1,0:T(8,128)} %collective-permute-done.1, f32[8,16,8192]{2,1,0:T(8,128)} %collective-permute-done, f32[3,8,16,8192]{3,2,0,1:T(8,128)S(1)} %convolution_bitcast_fusion.1, f32[2,8,16,8192]{3,2,1,0:T(8,128)} %param.6, f32[8,16]{1,0:T(8,128)S(1)} %add_add_fusion.1), kind=kLoop, calls=%fused_computation.25 | loop fusion | flops 4194304 | bytes 20972032 | tf_op jit(solution)/shard_map/broadcast_in_dim | solution.py:98
  139.8 86.8 %collective-permute-done.4 = f32[1,8,16,8192]{3,2,1,0:T(8,128)S(1)} collective-permute-done((f32[1,8,16,8192]{3,2,1,0:T(8,128)}, f32[1,8,16,8192]{3,2,1,0:T(8,128)S(1)}, u32[]{:S(2)}, u32[]{:S(2)}) %collective-permute-start.4) | collective-permute-done | bytes 4194336 | tf_op jit(solution)/shard_map/ppermute | solution.py:19
  226.6 4.0 collective-permute-done.5
  230.6 11.5 %fusion.4 = f32[96,8192]{1,0:T(8,128)} fusion(f32[8,3,16,96]{3,1,2,0:T(4,128)S(1)} %get-tuple-element.49, f32[1,8,16,8192]{3,2,1,0:T(8,128)S(1)} %collective-permute-done.5, f32[1,8,16,8192]{3,2,1,0:T(8,128)} %fusion.19, f32[1,8,16,8192]{3,2,1,0:T(8,128)S(1)} %collective-permute-done.4), kind=kOutput, calls=%fused_computation.8 | convolution fusion | flops 3630170112 | bytes 15876096 | tf_op jit(solution)/shard_map/aodz,oadc->zc/dot_general | solution.py:62
  249.0 9.5 %all-reduce.4 = (f32[96]{0:T(128)S(1)}, f32[96]{0:T(128)S(1)}) all-reduce(f32[96]{0:T(128)S(1)} %get-tuple-element.7, f32[96]{0:T(128)S(1)} %get-tuple-element.5), channel_id=1, replica_groups=mesh['tile'=32,'angle'=4] {'angle'}, use_global_device_ids=true, to_apply=%region_3.0 | all-reduce | flops 192 | bytes 1536 | tf_op jit(solution)/shard_map/psum | solution.py:68
  258.5 67.2 %all-reduce.8.cloned.1.call-done = f32[96,8192]{1,0:T(8,128)} async-done(((f32[96,8192]{1,0:T(8,128)}), f32[96,8192]{1,0:T(8,128)}) %all-reduce.8.cloned.1.call-update) | async-done | bytes 3145744 | tf_op jit(solution)/shard_map/psum | solution.py:68
  338.9 4.0 collective-permute-start.7
  342.9 4.1 rsqrt_multiply_fusion.5
  353.1 4.8 reshape.334
  357.9 11.9 %convolution_bitcast_fusion = f32[3,8,16,8192]{3,2,0,1:T(8,128)S(1)} fusion(f32[96,8192,1,1]{1,0,2,3:T(8,128)} %reshape.334, f32[8,3,16,96]{3,1,2,0:T(4,128)S(1)} %copy-done.4), kind=kOutput, calls=%fused_computation.6 | convolution fusion | flops 3623878656 | bytes 15876096 | tf_op jit(solution)/shard_map/aodz,zc->oadc/dot_general | solution.py:89
  372.5 5.2 collective-permute-start.8
  384.4 80.6 %collective-permute-done.10 = f32[8,16]{1,0:T(8,128)S(1)} collective-permute-done((f32[8,16]{1,0:T(8,128)S(1)}, f32[8,16]{1,0:T(8,128)S(1)}, u32[]{:S(2)}, u32[]{:S(2)}) %collective-permute-start.10) | collective-permute-done | bytes 544 | tf_op jit(solution)/shard_map/ppermute | solution.py:31
  465.0 5.6 collective-permute-done.11
  470.7 8.0 %fusion.14 = f32[1,8,16,8192]{3,2,1,0:T(8,128)} fusion(f32[8,16,8192]{2,1,0:T(8,128)} %collective-permute-done.9, f32[8,16,8192]{2,1,0:T(8,128)} %collective-permute-done.8, f32[3,8,16,8192]{3,2,0,1:T(8,128)S(1)} %convolution_bitcast_fusion, f32[2,8,16,8192]{3,2,1,0:T(8,128)} %param.6, f32[8,16]{1,0:T(8,128)S(1)} %add_add_fusion), kind=kLoop, calls=%fused_computation.17 | loop fusion | flops 4194304 | bytes 20972032 | tf_op jit(solution)/shard_map/broadcast_in_dim | solution.py:98
  483.6 86.7 %collective-permute-done.12 = f32[1,8,16,8192]{3,2,1,0:T(8,128)S(1)} collective-permute-done((f32[1,8,16,8192]{3,2,1,0:T(8,128)}, f32[1,8,16,8192]{3,2,1,0:T(8,128)S(1)}, u32[]{:S(2)}, u32[]{:S(2)}) %collective-permute-start.12) | collective-permute-done | bytes 4194336 | tf_op jit(solution)/shard_map/ppermute | solution.py:19
  570.3 4.0 collective-permute-done.13
  574.3 11.5 %fusion.7 = f32[96,8192]{1,0:T(8,128)} fusion(f32[8,3,16,96]{3,1,2,0:T(4,128)S(1)} %copy-done.4, f32[1,8,16,8192]{3,2,1,0:T(8,128)S(1)} %collective-permute-done.13, f32[1,8,16,8192]{3,2,1,0:T(8,128)} %fusion.14, f32[1,8,16,8192]{3,2,1,0:T(8,128)S(1)} %collective-permute-done.12), kind=kOutput, calls=%fused_computation.9 | convolution fusion | flops 3630170112 | bytes 15876096 | tf_op jit(solution)/shard_map/aodz,oadc->zc/dot_general | solution.py:62
  591.6 78.3 %all-reduce.10.cloned.1.call-done = f32[96,8192]{1,0:T(8,128)} async-done(((f32[96,8192]{1,0:T(8,128)}), f32[96,8192]{1,0:T(8,128)}) %all-reduce.10.cloned.1.call-update) | async-done | bytes 3145744 | tf_op jit(solution)/shard_map/psum | solution.py:68
  687.2 4.1 rsqrt_multiply_fusion.3
  (81 shorter events, 85.6 us)
Async XLA Ops:
  6.5 319.1 %all-reduce.8.cloned.1.call-start = ((), (), s32[]{:S(2)}) async-start(), calls=%async_computation | async-start | bytes 6291456 | tf_op jit(solution)/shard_map/psum | solution.py:68
  28.9 99.7 %collective-permute-start = (f32[8,16,8192]{2,1,0:T(8,128)}, f32[8,16,8192]{2,1,0:T(8,128)}, u32[]{:S(2)}, u32[]{:S(2)}) collective-permute-start(f32[8,16,8192]{2,1,0:T(8,128)} %get-tuple-element.19), channel_id=1, source_target_pairs={{0,4},{4,8},{8,12},{12,16},{16,20},{20,24},{24,28},{28,32},{32,36}... | collective-permute-start | bytes 12582920 | tf_op jit(solution)/shard_map/ppermute | solution.py:31
  35.2 93.4 %collective-permute-start.1 = (f32[8,16,8192]{2,1,0:T(8,128)S(1)}, f32[8,16,8192]{2,1,0:T(8,128)}, u32[]{:S(2)}, u32[]{:S(2)}) collective-permute-start(f32[8,16,8192]{2,1,0:T(8,128)S(1)} %get-tuple-element.20), channel_id=1, source_target_pairs={{4,0},{8,4},{12,8},{16,12},{20,16},{24,20},{28,24},{32,28},{36,32}... | collective-permute-start | bytes 12582920 | tf_op jit(solution)/shard_map/ppermute | solution.py:31
  36.9 85.9 %collective-permute-start.2 = (f32[8,16]{1,0:T(8,128)S(1)}, f32[8,16]{1,0:T(8,128)S(1)}, u32[]{:S(2)}, u32[]{:S(2)}) collective-permute-start(f32[8,16]{1,0:T(8,128)S(1)} %get-tuple-element.12), channel_id=1, source_target_pairs={{0,4},{4,8},{8,12},{12,16},{16,20},{20,24},{24,28},{28,32},{32,36}... | collective-permute-start | bytes 1544 | tf_op jit(solution)/shard_map/ppermute | solution.py:31
  40.9 87.7 %collective-permute-start.3 = (f32[8,16]{1,0:T(8,128)S(1)}, f32[8,16]{1,0:T(8,128)S(1)}, u32[]{:S(2)}, u32[]{:S(2)}) collective-permute-start(f32[8,16]{1,0:T(8,128)S(1)} %get-tuple-element.13), channel_id=1, source_target_pairs={{4,0},{8,4},{12,8},{16,12},{20,16},{24,20},{28,24},{32,28},{36,32}... | collective-permute-start | bytes 1544 | tf_op jit(solution)/shard_map/ppermute | solution.py:31
  136.7 89.9 %collective-permute-start.4 = (f32[1,8,16,8192]{3,2,1,0:T(8,128)}, f32[1,8,16,8192]{3,2,1,0:T(8,128)S(1)}, u32[]{:S(2)}, u32[]{:S(2)}) collective-permute-start(f32[1,8,16,8192]{3,2,1,0:T(8,128)} %fusion.19), channel_id=1, source_target_pairs={{0,4},{4,8},{8,12},{12,16},{16,20},{20,24},{24,28},{28,32},{32,36}... | collective-permute-start | bytes 12582920 | tf_op jit(solution)/shard_map/ppermute | solution.py:19
  138.5 92.1 %collective-permute-start.5 = (f32[1,8,16,8192]{3,2,1,0:T(8,128)}, f32[1,8,16,8192]{3,2,1,0:T(8,128)S(1)}, u32[]{:S(2)}, u32[]{:S(2)}) collective-permute-start(f32[1,8,16,8192]{3,2,1,0:T(8,128)} %fusion.19), channel_id=1, source_target_pairs={{4,0},{8,4},{12,8},{16,12},{20,16},{24,20},{28,24},{32,28},{36,32}... | collective-permute-start | bytes 12582920 | tf_op jit(solution)/shard_map/ppermute | solution.py:21
  242.1 1.9 copy-start.3
  242.1 427.7 %all-reduce.10.cloned.1.call-start = ((), (), s32[]{:S(2)}) async-start(), calls=%async_computation.1 | async-start | bytes 6291456 | tf_op jit(solution)/shard_map/psum | solution.py:68
  337.6 9.7 %collective-permute-start.6 = (f32[96,1,256]{2,1,0:T(1,128)S(1)}, f32[96,1,256]{2,1,0:T(1,128)S(1)}, u32[]{:S(2)}, u32[]{:S(2)}) collective-permute-start(f32[96,1,256]{2,1,0:T(1,128)S(1)} %get-tuple-element.31), channel_id=1, source_target_pairs={{4,0},{8,4},{12,8},{16,12},{20,16},{24,20},{28,24},{32,28},{36,32}... | collective-permute-start | bytes 294920 | tf_op jit(solution)/shard_map/ppermute | solution.py:21
  338.9 8.4 %collective-permute-start.7 = (f32[96,1,256]{2,1,0:T(1,128)S(1)}, f32[96,1,256]{2,1,0:T(1,128)S(1)}, u32[]{:S(2)}, u32[]{:S(2)}) collective-permute-start(f32[96,1,256]{2,1,0:T(1,128)S(1)} %get-tuple-element.32), channel_id=1, source_target_pairs={{0,4},{4,8},{8,12},{12,16},{16,20},{20,24},{24,28},{28,32},{32,36}... | collective-permute-start | bytes 294920 | tf_op jit(solution)/shard_map/ppermute | solution.py:19
  347.5 1.9 copy-start.2
  353.1 4.8 copy-start.4
  372.5 98.2 %collective-permute-start.8 = (f32[8,16,8192]{2,1,0:T(8,128)}, f32[8,16,8192]{2,1,0:T(8,128)}, u32[]{:S(2)}, u32[]{:S(2)}) collective-permute-start(f32[8,16,8192]{2,1,0:T(8,128)} %get-tuple-element.17), channel_id=1, source_target_pairs={{0,4},{4,8},{8,12},{12,16},{16,20},{20,24},{24,28},{28,32},{32,36}... | collective-permute-start | bytes 12582920 | tf_op jit(solution)/shard_map/ppermute | solution.py:31
  377.6 93.0 %collective-permute-start.9 = (f32[8,16,8192]{2,1,0:T(8,128)S(1)}, f32[8,16,8192]{2,1,0:T(8,128)}, u32[]{:S(2)}, u32[]{:S(2)}) collective-permute-start(f32[8,16,8192]{2,1,0:T(8,128)S(1)} %get-tuple-element.18), channel_id=1, source_target_pairs={{4,0},{8,4},{12,8},{16,12},{20,16},{24,20},{28,24},{32,28},{36,32}... | collective-permute-start | bytes 12582920 | tf_op jit(solution)/shard_map/ppermute | solution.py:31
  379.1 85.9 %collective-permute-start.10 = (f32[8,16]{1,0:T(8,128)S(1)}, f32[8,16]{1,0:T(8,128)S(1)}, u32[]{:S(2)}, u32[]{:S(2)}) collective-permute-start(f32[8,16]{1,0:T(8,128)S(1)} %get-tuple-element.9), channel_id=1, source_target_pairs={{0,4},{4,8},{8,12},{12,16},{16,20},{20,24},{24,28},{28,32},{32,36}... | collective-permute-start | bytes 1544 | tf_op jit(solution)/shard_map/ppermute | solution.py:31
  383.1 87.5 %collective-permute-start.11 = (f32[8,16]{1,0:T(8,128)S(1)}, f32[8,16]{1,0:T(8,128)S(1)}, u32[]{:S(2)}, u32[]{:S(2)}) collective-permute-start(f32[8,16]{1,0:T(8,128)S(1)} %get-tuple-element.10), channel_id=1, source_target_pairs={{4,0},{8,4},{12,8},{16,12},{20,16},{24,20},{28,24},{32,28},{36,32}... | collective-permute-start | bytes 1544 | tf_op jit(solution)/shard_map/ppermute | solution.py:31
  478.7 91.6 %collective-permute-start.12 = (f32[1,8,16,8192]{3,2,1,0:T(8,128)}, f32[1,8,16,8192]{3,2,1,0:T(8,128)S(1)}, u32[]{:S(2)}, u32[]{:S(2)}) collective-permute-start(f32[1,8,16,8192]{3,2,1,0:T(8,128)} %fusion.14), channel_id=1, source_target_pairs={{0,4},{4,8},{8,12},{12,16},{16,20},{20,24},{24,28},{28,32},{32,36}... | collective-permute-start | bytes 12582920 | tf_op jit(solution)/shard_map/ppermute | solution.py:19
  482.1 92.2 %collective-permute-start.13 = (f32[1,8,16,8192]{3,2,1,0:T(8,128)}, f32[1,8,16,8192]{3,2,1,0:T(8,128)S(1)}, u32[]{:S(2)}, u32[]{:S(2)}) collective-permute-start(f32[1,8,16,8192]{3,2,1,0:T(8,128)} %fusion.14), channel_id=1, source_target_pairs={{4,0},{8,4},{12,8},{16,12},{20,16},{24,20},{28,24},{32,28},{36,32}... | collective-permute-start | bytes 12582920 | tf_op jit(solution)/shard_map/ppermute | solution.py:21
  585.8 1.9 copy-start
  682.0 9.7 %collective-permute-start.14 = (f32[96,1,256]{2,1,0:T(1,128)S(1)}, f32[96,1,256]{2,1,0:T(1,128)S(1)}, u32[]{:S(2)}, u32[]{:S(2)}) collective-permute-start(f32[96,1,256]{2,1,0:T(1,128)S(1)} %get-tuple-element.25), channel_id=1, source_target_pairs={{4,0},{8,4},{12,8},{16,12},{20,16},{24,20},{28,24},{32,28},{36,32}... | collective-permute-start | bytes 294920 | tf_op jit(solution)/shard_map/ppermute | solution.py:21
  683.3 8.4 %collective-permute-start.15 = (f32[96,1,256]{2,1,0:T(1,128)S(1)}, f32[96,1,256]{2,1,0:T(1,128)S(1)}, u32[]{:S(2)}, u32[]{:S(2)}) collective-permute-start(f32[96,1,256]{2,1,0:T(1,128)S(1)} %get-tuple-element.26), channel_id=1, source_target_pairs={{0,4},{4,8},{8,12},{12,16},{16,20},{20,24},{24,28},{28,32},{32,36}... | collective-permute-start | bytes 294920 | tf_op jit(solution)/shard_map/ppermute | solution.py:19
  691.9 1.9 copy-start.1
Sparse Core Ops, SparseCore 0:
  242.3 83.3 all-reduce.7
  586.0 83.8 all-reduce.9
where the time goes:
time: 718 us; the launch traced here: 705 us
  waiting for transfers between devices  500 us (70%)
  matrix products  48.5 us (7%)
  local copies, waits for them, and re-layouts  47 us (7%)
  starting transfers between devices  43.9 us (6%)
  other arithmetic  42.2 us (6%)
  between operations  14.2 us (2%)
  blocking collectives  9.51 us (1%)
    ppermute x4, waiting for transfers between devices, padded_2(): lax.ppermute(tail, axis, [(i, (i + 1) % count) for i in range(ends)])  173 us
    ppermute x8, waiting for transfers between devices, passed_along(): lax.ppermute(value, axis, [(source, source + steps) for source in range(l...  173 us
    psum x2, waiting for transfers between devices, sum_angles(): return lax.psum((update, column_sums), 'angle')  145 us
    ppermute x8, starting transfers between devices, passed_along(): lax.ppermute(value, axis, [(source, source + steps) for source in range(l...  24.8 us
    dot_general x2, matrix products, per_device(): jnp.einsum('aodz,zc->oadc', combined, tile_cells, precision=lax.Precision...  23.8 us
    dot_general x2, matrix products, back_project(): jnp.einsum('aodz,oadc->zc', combined, nearby_resid, precision=lax.Precisi...  23 us
    broadcast_in_dim x2, other arithmetic, per_device(): nearby_resid = padded_2(residual[None], (('tile', 0),), 1)  16.1 us
    unnamed x16, local copies, waits for them, and re-layouts  15.8 us
  transfers between devices with their start and end apart: 18, of which 10 were waited for; matrix products, arithmetic and copies ran while one was open for 3% of the time, Pallas kernels for 0%

commit v1 on v0

v1 whole, which is shorter than its diff:
```python
import jax
import jax.numpy as jnp
from jax import lax
from jax.experimental import pallas as pl
from jax.experimental.pallas import tpu as pltpu
from jax.sharding import PartitionSpec as P

TV_WEIGHT = 0.05
TV_EPSILON = 0.01
MESH = pl.DeviceIdType.MESH
BF = jnp.bfloat16
F32 = jnp.float32

NZ, CY, QX = 96, 256, 8
QC = QX * CY
NC = 4
CH = QC // NC
NK = 4
ZK = NZ // NK
NA, DR, SLOTS = 8, 16, 3
ROWS = NA * DR


def split(value):
    hi = value.astype(BF)
    lo = (value - hi.astype(F32)).astype(BF)
    return hi, lo


def left_stack(value):
    hi, lo = split(value)
    return jnp.concatenate([hi, hi, lo], axis=1)


def right_stack(value):
    hi, lo = split(value)
    return jnp.concatenate([hi, lo, hi], axis=0)


def dot(a, b):
    return jnp.dot(a, b, preferred_element_type=F32)


def flux(difference):
    return difference * lax.rsqrt(difference * difference + TV_EPSILON)


def kernel(
    vol, meas, blk, ids, cnt, out,
    vq, xb, mb, ctb, csend, csb, gst, cst, po, pp, rz, rp, rsx, sp, xu, tvh, yq,
    lsem, s_w, r_w, s_ct, r_ct, s_cs, r_cs, s_m, r_m, s_h, r_h, s_z, r_z, s_p, r_p, s_x, r_x, s_t, r_t, s_o, r_o,
):
    t = lax.axis_index("tile")
    a = lax.axis_index("angle")
    nt = lax.axis_size("tile")
    h, c = a // 2, a % 2
    sib_a, xp_a, diag_a = 2 * h + 1 - c, (a + 2) % 4, 3 - a
    right_t, left_t = (t + 1) % nt, (t + nt - 1) % nt
    sib, xp, diag = (t, sib_a), (t, xp_a), (t, diag_a)
    sides = ((right_t, a), (left_t, a))
    g = t * 4 + a
    gr, gl = (g + 1) % (nt * 4), (g + nt * 4 - 1) % (nt * 4)
    tv_sides = ((gr // 4, gr % 4), (gl // 4, gl % 4))

    def remote(src, dst, ss, rs, dev):
        return pltpu.make_async_remote_copy(
            src_ref=src, dst_ref=dst, send_sem=ss, recv_sem=rs, device_id=dev, device_id_type=MESH
        )

    def vol_in():
        return pltpu.make_async_copy(vol.at[:, pl.ds(a * QX, QX), :], vq, lsem.at[0])

    def m_cols(k, core):
        return pl.ds((2 * k + core) * QC, QC)

    def m_in(s, k):
        return pltpu.make_async_copy(
            meas.at[s, :, :, m_cols(k, c)], mb.at[s, k, pl.ds(c * NA, NA)], lsem.at[1 + 2 * s + k]
        )

    def m_sib(s, k):
        return remote(
            meas.at[s, :, :, m_cols(k, 1 - c)], mb.at[s, k, pl.ds(c * NA, NA)],
            s_m.at[s, k], r_m.at[s, k], sib,
        )

    def w_side(s, d):
        return remote(csend.at[s, d], ctb.at[a, s, 2 * d], s_w.at[s, d], r_w.at[s, d], sides[d])

    def ct_sib(s):
        return remote(ctb.at[a, s], ctb.at[a, s], s_ct.at[0, s], r_ct.at[0, s], sib)

    def ct_xp(s):
        return remote(ctb.at[a, s], ctb.at[a, s], s_ct.at[1, s], r_ct.at[1, s], xp)

    def ct_fwd(s):
        return remote(ctb.at[xp_a, s], ctb.at[xp_a, s], s_ct.at[2, s], r_ct.at[2, s], sib)

    def cs_to(i):
        return remote(csb.at[a], csb.at[a], s_cs.at[i], r_cs.at[i], (sib, xp, diag)[i])

    def halo(s, d, j):
        return remote(xb.at[s, 1, j], xb.at[s, 2 * d, j], s_h.at[s, d, j], r_h.at[s, d, j], sides[d])

    def z_own(s, d, j):
        return remote(po.at[s, 2 - 2 * d, j], rz.at[s, d, j], s_z.at[s, d, j], r_z.at[s, d, j], sides[d])

    def z_part(s, d, j):
        return remote(pp.at[s, 2 - 2 * d, j], rp.at[s, d, j], s_p.at[s, d, j], r_p.at[s, d, j], sides[d])

    def x_sum(s, j):
        return remote(sp.at[s, j], rsx.at[s, j], s_x.at[s, j], r_x.at[s, j], xp)

    def tv_side(s, d):
        src = xu.at[s, NC - 1, :, pl.ds(CH - CY, CY)] if d == 0 else xu.at[s, 0, :, pl.ds(0, CY)]
        return remote(src, tvh.at[s, d], s_t.at[s, d], r_t.at[s, d], tv_sides[d])

    def out_at(k, q):
        return out.at[pl.ds(k * ZK, ZK), pl.ds(q * QX, QX), :]

    def out_own(k):
        return pltpu.make_async_copy(yq.at[pl.ds(k * ZK, ZK)], out_at(k, a), lsem.at[5 + k])

    def out_to(i, k):
        return remote(yq.at[pl.ds(k * ZK, ZK)], out_at(k, a), s_o.at[i, k], r_o.at[i, k], (sib, xp)[i])

    def out_fwd(k):
        return remote(out_at(k, xp_a), out_at(k, xp_a), s_o.at[2, k], r_o.at[2, k], sib)

    def loop(count, body):
        def step(i, carry):
            body(i)
            return carry

        lax.fori_loop(0, count, step, 0)

    vol_in().start()
    for s in range(2):
        for k in range(2):
            m_in(s, k).start()
    peers = (sib, xp, diag) + sides + tv_sides
    barrier = pltpu.get_barrier_semaphore()
    for peer in peers:
        pl.semaphore_signal(barrier, inc=1, device_id=peer, device_id_type=MESH)

    for s in range(2):
        sums = jnp.zeros((1, NZ), F32)
        for o in range(3):
            rows = []
            for n in range(NA):
                block = jnp.zeros((DR, NZ), F32)
                for k in range(SLOTS):
                    live = (cnt[s, n, 0] > k) & (ids[s, n, k] - t == o - 1)
                    block = block + blk[s, n, k] * jnp.where(live, 1.0, 0.0).astype(F32)
                rows.append(block)
            block = jnp.concatenate(rows, axis=0)
            sums = sums + jnp.sum(block, axis=0, keepdims=True)
            turned = block.T
            if o == 1:
                ctb[a, s, 1] = turned
            else:
                csend[s, 1 - o // 2] = turned
        csb[a, s] = jnp.broadcast_to(jnp.concatenate([sums, jnp.ones((1, 128 - NZ), F32)], axis=1), (8, 128))

    pl.semaphore_wait(barrier, len(peers))

    for d in range(2):
        w_side(0, d).start()
    for k in range(2):
        m_sib(0, k).start()
    for i in range(3):
        cs_to(i).start()
    vol_in().wait()
    for x in range(QX):
        xb[0, 1, x * CY // CH, :, pl.ds(x * CY % CH, CY)] = vq[:, x, :]
    for j in range(NC):
        for d in range(2):
            halo(0, d, j).start()
    for d in range(2):
        w_side(1, d).start()
    for k in range(2):
        m_sib(1, k).start()

    def weights_on(s):
        for d in range(2):
            w_side(s, d).wait_recv()
        ct_sib(s).start()
        ct_xp(s).start()

    def back_data(s):
        ct_sib(s).wait_recv()
        for k in range(2):
            m_in(s, k).wait()
            m_sib(s, k).wait_recv()
        ct = jnp.concatenate(
            [ctb[2 * h + k, s].reshape(3 * NZ, ROWS) for k in range(2)], axis=1
        )
        cst[s] = left_stack(ct / jnp.sum(ct, axis=0, keepdims=True))

        def chunk(j):
            cols = pl.ds(pl.multiple_of(j * CH, CH), CH)
            for k, target in ((1 - h, pp), (h, po)):
                rows = mb[s, k, :, :, cols].reshape(2 * ROWS, CH)
                prod = dot(cst[s], right_stack(rows))
                for o in range(3):
                    target[s, o, j] = prod[o * NZ:(o + 1) * NZ]
                if target is pp:
                    for d in range(2):
                        z_part(s, d, j).start()

        loop(NC, chunk)

    def operator(s):
        ct_xp(s).wait_recv()
        ct_fwd(s).start()
        ct_fwd(s).wait_recv()
        ct = jnp.concatenate([ctb[q, s].reshape(3 * NZ, ROWS) for q in range(4)], axis=1)
        scaled = ct / jnp.sum(ct, axis=0, keepdims=True)
        gram = lax.dot_general(
            scaled, ct, (((1,), (1,)), ((), ())),
            precision=lax.Precision.HIGHEST, preferred_element_type=F32,
        )
        gst[s] = left_stack(gram)

    def own_chunk(s, j):
        for d in range(2):
            halo(s, d, j).wait_recv()
        prod = dot(gst[s], right_stack(xb[s, :, j].reshape(3 * NZ, CH)))
        for o in range(3):
            po[s, o, j] = po[s, o, j] - prod[o * NZ:(o + 1) * NZ]
        for d in range(2):
            z_own(s, d, j).start()

    def part_chunk(s, j):
        for d in range(2):
            z_part(s, d, j).wait_recv()
        sp[s, j] = pp[s, 1, j] + rp[s, 0, j] + rp[s, 1, j]
        x_sum(s, j).start()

    def scale(s):
        sums = csb[0, s] + csb[1, s] + csb[2, s] + csb[3, s]
        square = jnp.broadcast_to(sums[:1], (128, 128)).T[:NZ]
        return 1.0 / square

    def update_chunk(s, j, inverse):
        for d in range(2):
            z_own(s, d, j).wait_recv()
        x_sum(s, j).wait_recv()
        total = po[s, 1, j] + rz[s, 0, j] + rz[s, 1, j] + rsx[s, j]
        xu[s, j] = xb[s, 1, j] + total * jnp.concatenate([inverse] * (CH // 128), axis=1)

    z_pos = lax.broadcasted_iota(jnp.int32, (NZ, CY), 0)
    y_pos = lax.broadcasted_iota(jnp.int32, (NZ, CY), 1)

    def inner_term(cur, axis, pos):
        extent = cur.shape[axis]
        ahead = pltpu.roll(cur, extent - 1, axis)
        f = flux(jnp.where(pos == extent - 1, 0.0, ahead - cur))
        return pltpu.roll(f, 1, axis) - f

    def x_row(s, x):
        return xu[s, x * CY // CH, :, pl.ds(x * CY % CH, CY)]

    def smooth(s, store):
        for d in range(2):
            tv_side(s, d).wait_recv()
        first, last = x_row(s, 0), x_row(s, QX - 1)
        left = jnp.where(g == 0, first, tvh[s, 0])
        right = jnp.where(g == nt * 4 - 1, last, tvh[s, 1])
        before = flux(first - left)
        for x in range(QX):
            cur = x_row(s, x)
            ahead = x_row(s, x + 1) if x < QX - 1 else right
            after = flux(ahead - cur)
            term = (before - after) + inner_term(cur, 0, z_pos) + inner_term(cur, 1, y_pos)
            store(x, cur - TV_WEIGHT * term)
            before = after

    def store_next(x, value):
        j = x * CY // CH
        xb[1, 1, j, :, pl.ds(x * CY % CH, CY)] = value
        if (x + 1) * CY % CH == 0:
            for d in range(2):
                halo(1, d, j).start()

    def store_last(x, value):
        yq[:, x, :] = value

    weights_on(0)
    back_data(0)
    operator(0)

    def both(j):
        own_chunk(0, j)
        part_chunk(0, j)

    loop(NC, both)
    weights_on(1)
    back_data(1)
    operator(1)
    for i in range(3):
        cs_to(i).wait_recv()
    inverse = scale(0)
    for j in (0, NC - 1, *range(1, NC - 1)):
        update_chunk(0, j, inverse)
        if j == 0:
            tv_side(0, 1).start()
        if j == NC - 1:
            tv_side(0, 0).start()
    smooth(0, store_next)

    loop(NC, lambda j: part_chunk(1, j))
    loop(NC, lambda j: own_chunk(1, j))
    inverse = scale(1)
    for j in (0, NC - 1, *range(1, NC - 1)):
        update_chunk(1, j, inverse)
        if j == 0:
            tv_side(1, 1).start()
        if j == NC - 1:
            tv_side(1, 0).start()
    smooth(1, store_last)

    for k in range(NK):
        out_to(1, k).start()
    for k in range(NK):
        out_to(0, k).start()
        out_own(k).start()
    for k in range(NK):
        out_to(1, k).wait_recv()
        out_fwd(k).start()
    for k in range(NK):
        out_to(0, k).wait_recv()
        out_fwd(k).wait_recv()
        out_own(k).wait()
        out_fwd(k).wait_send()
        for i in range(2):
            out_to(i, k).wait_send()

    for s in range(2):
        for d in range(2):
            w_side(s, d).wait_send()
            tv_side(s, d).wait_send()
        for k in range(2):
            m_sib(s, k).wait_send()
        ct_sib(s).wait_send()
        ct_xp(s).wait_send()
        ct_fwd(s).wait_send()

        def drain(j, s=s):
            for d in range(2):
                halo(s, d, j).wait_send()
                z_own(s, d, j).wait_send()
                z_part(s, d, j).wait_send()
            x_sum(s, j).wait_send()

        loop(NC, drain)
    for i in range(3):
        cs_to(i).wait_send()


def per_device(volume, measured, blocks, ray_lists, counts):
    vmem, smem, anywhere = (
        pl.BlockSpec(memory_space=space) for space in (pltpu.VMEM, pltpu.SMEM, pl.ANY)
    )
    dma = pltpu.SemaphoreType.DMA
    return pl.pallas_call(
        kernel,
        out_shape=jax.ShapeDtypeStruct(volume.shape, F32),
        in_specs=[anywhere, anywhere, vmem, smem, smem],
        out_specs=anywhere,
        scratch_shapes=[
            pltpu.VMEM((NZ, QX, CY), F32),
            pltpu.VMEM((2, 3, NC, NZ, CH), F32),
            pltpu.VMEM((2, 2, 2 * NA, DR, QC), F32),
            pltpu.VMEM((4, 2, 3, NZ, ROWS), F32),
            pltpu.VMEM((2, 2, NZ, ROWS), F32),
            pltpu.VMEM((4, 2, 8, 128), F32),
            pltpu.VMEM((2, 3 * NZ, 9 * NZ), BF),
            pltpu.VMEM((2, 3 * NZ, 6 * ROWS), BF),
            pltpu.VMEM((2, 3, NC, NZ, CH), F32),
            pltpu.VMEM((2, 3, NC, NZ, CH), F32),
            pltpu.VMEM((2, 2, NC, NZ, CH), F32),
            pltpu.VMEM((2, 2, NC, NZ, CH), F32),
            pltpu.VMEM((2, NC, NZ, CH), F32),
            pltpu.VMEM((2, NC, NZ, CH), F32),
            pltpu.VMEM((2, NC, NZ, CH), F32),
            pltpu.VMEM((2, 2, NZ, CY), F32),
            pltpu.VMEM((NZ, QX, CY), F32),
            dma((5 + NK,)),
            dma((2, 2)), dma((2, 2)),
            dma((3, 2)), dma((3, 2)),
            dma((3,)), dma((3,)),
            dma((2, 2)), dma((2, 2)),
            dma((2, 2, NC)), dma((2, 2, NC)),
            dma((2, 2, NC)), dma((2, 2, NC)),
            dma((2, 2, NC)), dma((2, 2, NC)),
            dma((2, NC)), dma((2, NC)),
            dma((2, 2)), dma((2, 2)),
            dma((3, NK)), dma((3, NK)),
        ],
        compiler_params=pltpu.CompilerParams(
            collective_id=0, has_side_effects=True, vmem_limit_bytes=56 * 1024 * 1024
        ),
        name="sart_tv",
    )(volume, measured, blocks, ray_lists, counts)


def solution(mesh):
    return jax.shard_map(
        per_device,
        mesh=mesh,
        in_specs=(
            P(None, "tile", None),
            P(None, "angle", "tile", None),
            P(None, "angle", "tile", None, None),
            P(None, "angle", "tile"),
            P(None, "angle", "tile"),
        ),
        out_specs=P(None, "tile", None),
        check_vma=False,
    )
```

time: 718 us -> 191 us (0.27); the launches traced: 705 us -> 190 us
  waiting for transfers between devices: 500 us -> 0 us
  Pallas kernels: 0 us -> 183 us
  matrix products: 48.5 us -> 0 us
  starting transfers between devices: 43.9 us -> 0 us
  other arithmetic: 42.2 us -> 0 us
  local copies, waits for them, and re-layouts: 47 us -> 6.68 us
  between operations: 14.2 us -> 0.01 us
  blocking collectives: 9.51 us -> 0 us
    ppermute x16 -> x0, waiting for transfers between devices: 354 us -> none  [the longest x4 173 us: padded_2(): lax.ppermute(tail, axis, [(i, (i + 1) % count) for i in range(ends)])]
    pallas_call x0 -> x1, Pallas kernels: none -> 183 us  [per_device(): pl.pallas_call(kernel, out_shape=jax.ShapeDtypeStruct(volume.shape, F32),...]
    psum x2 -> x0, waiting for transfers between devices: 145 us -> none  [sum_angles(): return lax.psum((update, column_sums), 'angle')]
    dot_general x6 -> x0, matrix products: 48.5 us -> none  [the longest x2 23.8 us: per_device(): jnp.einsum('aodz,zc->oadc', combined, tile_cells, precision=lax.Precision...]
    ppermute x16 -> x0, starting transfers between devices: 43.4 us -> none  [the longest x8 24.8 us: passed_along(): lax.ppermute(value, axis, [(source, source + steps) for source in range(l...]
    broadcast_in_dim x2 -> x0, other arithmetic: 16.1 us -> none  [per_device(): nearby_resid = padded_2(residual[None], (('tile', 0),), 1)]
    slice x19 -> x0, local copies, waits for them, and re-layouts: 15.6 us -> none  [the longest x6 9.71 us: direction_term(): lax.slice_in_dim(volume, 1, extent, axis=axis_pos)]
    div x4 -> x0, other arithmetic: 10.8 us -> none  [the longest x2 8.23 us: direction_term(): fluxes = difference / jnp.sqrt(difference * difference + TV_EPSILON)]
  transfers between devices with their start and end apart: 18 -> 0, of which waited for: 10 -> 0; matrix products, arithmetic and copies ran while one was open for 3% -> 0% of each run, Pallas kernels for 0% -> 0%
where the time goes in v1:
time: 191 us; the launch traced here: 190 us
  Pallas kernels  183 us (96%)
  local copies, waits for them, and re-layouts  6.68 us (3%)
    pallas_call x1, Pallas kernels, per_device(): pl.pallas_call(kernel, out_shape=jax.ShapeDtypeStruct(volume.shape, F32),...  183 us
    unnamed x3, local copies, waits for them, and re-layouts  6.68 us

profile of v1, /device:TPU:1, one launch (start us, length us, event | category | flops | bytes accessed | tf_op | source)
XLA Modules:
  0.0 189.9 jit_solution(787255602717566583)
XLA Ops:
  0.0 1.4 copy.6.ids
  1.4 1.4 copy.7.cnt
  2.7 183.2 %sart_tv.1 = f32[96,32,256]{2,1,0:T(8,128)} custom-call(f32[96,32,256]{2,1,0:T(8,128)} %vol.1, f32[2,8,16,8192]{3,2,1,0:T(8,128)} %meas.1, f32[2,8,3,16,96]{4,3,2,1,0:T(8,128)} %blk.1, s32[2,8,3]{2,1,0:T(8,128)} %copy.6.ids, s32[2,8,1]{2,1,0:T(8,128)} %copy.7.cnt), custom_call_target="tpu_custom_call" | custom-call | tf_op jit(solution)/shard_map/sart_tv/pallas_call | solution.py:366
  185.9 4.0 %copy.9 = f32[96,32,256]{2,1,0:T(8,128)} copy(f32[96,32,256]{2,1,0:T(8,128)} %sart_tv.1) | data formatting | bytes 6291456

commit v2 on v1

v2 whole, which is shorter than its diff:
```python
import jax
import jax.numpy as jnp
from jax import lax
from jax.experimental import pallas as pl
from jax.experimental.pallas import tpu as pltpu
from jax.sharding import PartitionSpec as P

TV_WEIGHT = 0.05
TV_EPSILON = 0.01
MESH = pl.DeviceIdType.MESH
BF = jnp.bfloat16
F32 = jnp.float32

NZ, CY, TX = 96, 256, 32
UX = 4
UC = UX * CY
NC = 4
CH = 2 * UC // NC
UNC = NC // 2
EARLY = 2
RUN = 4
NA, DR, SLOTS = 8, 16, 3
ROWS = NA * DR


def split(value):
    hi = value.astype(BF)
    lo = (value - hi.astype(F32)).astype(BF)
    return hi, lo


def left_stack(value):
    hi, lo = split(value)
    return jnp.concatenate([hi, hi, lo], axis=1)


def right_stack(value):
    hi, lo = split(value)
    return jnp.concatenate([hi, lo, hi], axis=0)


def dot(a, b):
    return jnp.dot(a, b, preferred_element_type=F32)


def flux(difference):
    return difference * lax.rsqrt(difference * difference + TV_EPSILON)


def kernel(
    vol, meas, blk, ids, cnt, out,
    vq, xb, mb, ctb, csend, csb, gst, cst, po, pp, rz, rp, rsx, sp, xu, tvh, xall, edge, yt,
    lsem, s_w, r_w, s_ct, r_ct, s_cs, r_cs, s_m, r_m, s_h, r_h, s_z, r_z, s_p, r_p, s_x, r_x, s_t, r_t, s_o, r_o, s_e, r_e,
):
    t = lax.axis_index("tile")
    a = lax.axis_index("angle")
    nt = lax.axis_size("tile")
    h, c = a // 2, a % 2
    sib_a, xp_a, diag_a = 2 * h + 1 - c, (a + 2) % 4, 3 - a
    right_t, left_t = (t + 1) % nt, (t + nt - 1) % nt
    sib, xp, diag = (t, sib_a), (t, xp_a), (t, diag_a)
    ends = ((t % RUN) // (RUN - 1), ((t + RUN - 1) % RUN) // (RUN - 1))
    x_lo = (t // RUN) % 2
    x_lo_left = (left_t // RUN) % 2

    def upper(angle, u):
        return (u + angle) % 2

    def side(d, u=None):
        turn = 0 if u is None else 2 * upper(a, u) * ends[d]
        return ((right_t, left_t)[d], (a + turn) % 4)

    def region(angle, u):
        up = upper(angle, u)
        return (1 - up) * angle + up * (4 + (angle + 2 * x_lo) % 4)

    b = (a + 2 * x_lo) % 4
    top, low = a // 3, 1 - (a + 3) // 4
    top_b, low_b = b // 3, 1 - (b + 3) // 4
    owners = (
        (
            (t, (1 - top) * ((a + 1) % 4) + top * (2 * x_lo), top),
            ((1 - top_b) * t + top_b * right_t, (1 - top_b) * ((a + 1) % 4), 1 - top_b),
        ),
        (
            ((1 - low) * t + low * left_t, (1 - low) * ((a + 3) % 4) + low * ((3 + 2 * x_lo_left) % 4), low),
            (t, (1 - low_b) * ((a + 3) % 4) + low_b * 3, 1 - low_b),
        ),
    )

    def beside(d, u):
        up = upper(a, u)
        tile, angle, there = (
            (1 - up) * low_one + up * up_one for low_one, up_one in zip(owners[d][0], owners[d][1])
        )
        return tile, angle, (there + angle) % 2

    def remote(src, dst, ss, rs, dev):
        return pltpu.make_async_remote_copy(
            src_ref=src, dst_ref=dst, send_sem=ss, recv_sem=rs, device_id=dev, device_id_type=MESH
        )

    def vol_in(u):
        rows = pl.ds(pl.multiple_of(region(a, u) // 2 * 8, 8), 8)
        return pltpu.make_async_copy(vol.at[:, rows, :], vq.at[u], lsem.at[u])

    def m_cols(angle, u):
        return pl.ds(pl.multiple_of(region(angle, u) * UC, UC), UC)

    def m_in(s, k, u):
        return pltpu.make_async_copy(
            meas.at[s, :, :, m_cols((a, xp_a)[k], u)], mb.at[s, k, u, pl.ds(c * NA, NA)],
            lsem.at[2 + 4 * s + 2 * k + u],
        )

    def m_sib(s, k, u):
        return remote(
            meas.at[s, :, :, m_cols((sib_a, diag_a)[k], u)], mb.at[s, k, u, pl.ds(c * NA, NA)],
            s_m.at[s, k, u], r_m.at[s, k, u], sib,
        )

    def w_side(s, d):
        return remote(csend.at[s, d], ctb.at[a, s, 2 * d], s_w.at[s, d], r_w.at[s, d], side(d))

    def ct_sib(s):
        return remote(ctb.at[a, s], ctb.at[a, s], s_ct.at[0, s], r_ct.at[0, s], sib)

    def ct_xp(s):
        return remote(ctb.at[a, s], ctb.at[a, s], s_ct.at[1, s], r_ct.at[1, s], xp)

    def ct_fwd(s):
        return remote(ctb.at[xp_a, s], ctb.at[xp_a, s], s_ct.at[2, s], r_ct.at[2, s], sib)

    def cs_to(i):
        return remote(csb.at[a], csb.at[a], s_cs.at[i], r_cs.at[i], (sib, xp, diag)[i])

    def halo(s, d, j):
        return remote(xb.at[s, 1, j], xb.at[s, 2 * d, j], s_h.at[s, d, j], r_h.at[s, d, j], side(d, j // UNC))

    def z_own(s, d, j):
        return remote(po.at[s, 2 - 2 * d, j], rz.at[s, d, j], s_z.at[s, d, j], r_z.at[s, d, j], side(d, j // UNC))

    def z_part(s, d, j):
        return remote(pp.at[s, 2 - 2 * d, j], rp.at[s, d, j], s_p.at[s, d, j], r_p.at[s, d, j], side(d, j // UNC))

    def x_sum(s, j):
        return remote(sp.at[s, j], rsx.at[s, j], s_x.at[s, j], r_x.at[s, j], xp)

    def tv_side(d, u):
        src = x_ref(u, UX - 1) if d == 0 else x_ref(u, 0)
        tile, angle, slot = beside(d, u)
        return remote(src, tvh.at[d, slot], s_t.at[d, u], r_t.at[d, slot], (tile, angle))

    def tv_from(d, u):
        return remote(tvh.at[d, u], tvh.at[d, u], s_t.at[d, u], r_t.at[d, u], sib)

    def x_ref(u, x):
        return xu.at[u * UNC + x * CY // CH, :, pl.ds(x * CY % CH, CY)]

    def x_row(u, x):
        return x_ref(u, x)[...]

    def whole_at(angle, j):
        return xall.at[region(angle, j // UNC), j % UNC]

    def whole_to(i, j):
        return remote(whole_at(a, j), whole_at(a, j), s_o.at[i, j], r_o.at[i, j], (sib, xp)[i])

    def whole_fwd(j):
        return remote(whole_at(xp_a, j), whole_at(xp_a, j), s_o.at[2, j], r_o.at[2, j], sib)

    def whole_ref(x):
        return xall.at[x // UX, x % UX * CY // CH, :, pl.ds(x * CY % CH, CY)]

    def edge_to(d):
        return remote(whole_ref((1 - d) * (TX - 1)), edge.at[d], s_e.at[d], r_e.at[d], side(d))

    def out_rows(k):
        rows = pl.ds(8 * k, 8)
        return pltpu.make_async_copy(yt.at[:, rows, :], out.at[:, rows, :], lsem.at[10 + k])

    def loop(count, body):
        def step(i, carry):
            body(i)
            return carry

        lax.fori_loop(0, count, step, 0)

    for u in range(2):
        vol_in(u).start()
    for s in range(2):
        for k in (1, 0):
            for u in range(2):
                m_in(s, k, u).start()
    peers = (sib, xp, diag) + tuple(side(d, u) for d in range(2) for u in range(2))
    peers = peers + tuple(beside(d, u)[:2] for d in range(2) for u in range(2))
    barrier = pltpu.get_barrier_semaphore()
    for peer in peers:
        pl.semaphore_signal(barrier, inc=1, device_id=peer, device_id_type=MESH)

    def own_weights(s):
        sums = jnp.zeros((1, NZ), F32)
        for o in range(3):
            rows = []
            for n in range(NA):
                block = jnp.zeros((DR, NZ), F32)
                for k in range(SLOTS):
                    live = (cnt[s, n, 0] > k) & (ids[s, n, k] - t == o - 1)
                    block = block + blk[s, n, k] * jnp.where(live, 1.0, 0.0).astype(F32)
                rows.append(block)
            block = jnp.concatenate(rows, axis=0)
            sums = sums + jnp.sum(block, axis=0, keepdims=True)
            turned = block.T
            if o == 1:
                ctb[a, s, 1] = turned
            else:
                csend[s, 1 - o // 2] = turned
        csb[a, s] = jnp.broadcast_to(jnp.concatenate([sums, jnp.ones((1, 128 - NZ), F32)], axis=1), (8, 128))

    def send_m(s):
        for k in (1, 0):
            for u in range(2):
                m_sib(s, k, u).start()

    def slab_in(u):
        vol_in(u).wait()
        first_row = region(a, u) % 2 * UX
        for x in range(UX):
            xb[0, 1, u * UNC + x * CY // CH, :, pl.ds(x * CY % CH, CY)] = vq[u, :, first_row + x, :]

    def send_halo(s, j):
        for d in range(2):
            halo(s, d, j).start()

    def send_weights(s):
        for d in range(2):
            w_side(s, d).start()

    own_weights(0)
    slab_in(0)
    pl.semaphore_wait(barrier, len(peers))
    send_weights(0)
    send_m(0)
    send_halo(0, 0)
    send_halo(0, 1)
    own_weights(1)
    send_weights(1)
    for i in range(3):
        cs_to(i).start()
    slab_in(1)

    def weights_on(s):
        for d in range(2):
            w_side(s, d).wait_recv()
        ct_sib(s).start()
        ct_xp(s).start()

    def back_weights(s):
        ct_sib(s).wait_recv()
        ct = jnp.concatenate(
            [ctb[2 * h + k, s].reshape(3 * NZ, ROWS) for k in range(2)], axis=1
        )
        cst[s] = left_stack(ct / jnp.sum(ct, axis=0, keepdims=True))

    def back_data(s, k):
        target = pp if k == 1 else po
        for u in range(2):
            m_in(s, k, u).wait()
            m_sib(s, k, u).wait_recv()

        def chunk(j):
            cols = pl.ds(pl.multiple_of(j % UNC * CH, CH), CH)
            rows = mb[s, k, j // UNC, :, :, cols].reshape(2 * ROWS, CH)
            prod = dot(cst[s], right_stack(rows))
            for o in range(3):
                target[s, o, j] = prod[o * NZ:(o + 1) * NZ]
            if k == 1 and s == 0:
                for d in range(2):
                    z_part(s, d, j).start()

        loop(NC, chunk)

    def send_part(s, j):
        for d in range(2):
            z_part(s, d, j).start()

    def operator(s):
        ct_xp(s).wait_recv()
        ct_fwd(s).start()
        ct_fwd(s).wait_recv()
        ct = jnp.concatenate([ctb[q, s].reshape(3 * NZ, ROWS) for q in range(4)], axis=1)
        scaled = ct / jnp.sum(ct, axis=0, keepdims=True)
        gram = lax.dot_general(
            scaled, ct, (((1,), (1,)), ((), ())),
            precision=lax.Precision.HIGHEST, preferred_element_type=F32,
        )
        gst[s] = left_stack(gram)

    def own_chunk(s, j):
        for d in range(2):
            halo(s, d, j).wait_recv()
        prod = dot(gst[s], right_stack(xb[s, :, j].reshape(3 * NZ, CH)))
        for o in range(3):
            po[s, o, j] = po[s, o, j] - prod[o * NZ:(o + 1) * NZ]
        for d in range(2):
            z_own(s, d, j).start()

    def part_chunk(s, j):
        for d in range(2):
            z_part(s, d, j).wait_recv()
        sp[s, j] = pp[s, 1, j] + rp[s, 0, j] + rp[s, 1, j]
        x_sum(s, j).start()

    def scale(s):
        sums = csb[0, s] + csb[1, s] + csb[2, s] + csb[3, s]
        square = jnp.broadcast_to(sums[:1], (128, 128)).T[:NZ]
        return 1.0 / square

    def update_chunk(s, j, inverse):
        for d in range(2):
            z_own(s, d, j).wait_recv()
        x_sum(s, j).wait_recv()
        total = po[s, 1, j] + rz[s, 0, j] + rz[s, 1, j] + rsx[s, j]
        updated = xb[s, 1, j] + total * jnp.concatenate([inverse] * (CH // 128), axis=1)
        if s == 0:
            xu[j] = updated
        else:
            whole_at(a, j)[...] = updated

    z_pos = lax.broadcasted_iota(jnp.int32, (NZ, CY), 0)
    y_pos = lax.broadcasted_iota(jnp.int32, (NZ, CY), 1)

    def inner_term(cur, axis, pos):
        extent = cur.shape[axis]
        ahead = pltpu.roll(cur, extent - 1, axis)
        f = flux(jnp.where(pos == extent - 1, 0.0, ahead - cur))
        return pltpu.roll(f, 1, axis) - f

    def smooth_row(cur, left, right):
        term = flux(cur - left) - flux(right - cur) + inner_term(cur, 0, z_pos) + inner_term(cur, 1, y_pos)
        return cur - TV_WEIGHT * term

    def store_next(u, x, left, right):
        j = u * UNC + x * CY // CH
        xb[1, 1, j, :, pl.ds(x * CY % CH, CY)] = smooth_row(x_row(u, x), left, right)

    def first_step():
        inverse = scale(0)
        for j in range(NC):
            update_chunk(0, j, inverse)
            if j % UNC == 0:
                tv_side(1, j // UNC).start()
            else:
                tv_side(0, j // UNC).start()
        for j in range(EARLY, NC):
            send_part(1, j)
        for u in range(2):
            for x in range(1, UX - 1):
                store_next(u, x, x_row(u, x - 1), x_row(u, x + 1))
        for j in range(EARLY):
            part_chunk(1, j)
        for j in range(NC):
            u, x = j // UNC, j % UNC * (UX - 1)
            d = 0 if x == 0 else 1
            tv_from(d, u).wait_recv()
            cur, rim = x_row(u, x), tvh[d, u]
            if d == 0:
                rim = jnp.where((t == 0) & (region(a, u) == 0), cur, rim)
                store_next(u, x, rim, x_row(u, x + 1))
            else:
                rim = jnp.where((t == nt - 1) & (region(a, u) == 7), cur, rim)
                store_next(u, x, x_row(u, x - 1), rim)
            send_halo(1, j)

    def whole_row(x):
        return whole_ref(x)[...]

    def whole_here(j):
        whole_to(0, j).wait_recv()
        whole_fwd(j).wait_recv()

    def last_row(x):
        cur = whole_row(x)
        left = whole_row(x - 1) if x > 0 else jnp.where(t == 0, cur, edge[0])
        right = whole_row(x + 1) if x < TX - 1 else jnp.where(t == nt - 1, cur, edge[1])
        yt[:, x, :] = smooth_row(cur, left, right)

    def last_step():
        inverse = scale(1)

        def pass_on(j):
            whole_to(1, j).wait_recv()
            whole_fwd(j).start()

        def update(j):
            update_chunk(1, j, inverse)
            whole_to(1, j).start()
            whole_to(0, j).start()

        done = set()

        def rows_of(first):
            for x in range(first * UX, first * UX + UX):
                if x not in done and all(
                    n in (-1, TX) or (n // UX) in ready for n in (x - 1, x + 1)
                ):
                    done.add(x)
                    last_row(x)
            k = first * UX // 8
            if all(x in done for x in range(8 * k, 8 * k + 8)):
                out_rows(k).start()

        update(0)
        update(1)
        pass_on(0)
        update(2)
        pass_on(1)
        whole_here(0)
        edge_to(1).start()
        whole_here(1)
        edge_to(0).start()
        update(3)
        pass_on(2)
        ready = (0, 2, 5, 7)
        for d in range(2):
            edge_to(d).wait_recv()
        for e in ready:
            rows_of(e)
        pass_on(3)
        for j in range(UNC, NC):
            whole_here(j)
        ready = range(TX // UX)
        for e in ready:
            rows_of(e)

    weights_on(0)
    back_weights(0)
    back_data(0, 1)
    send_halo(0, 2)
    send_halo(0, 3)
    send_m(1)
    back_data(0, 0)
    weights_on(1)
    operator(0)
    for j in range(UNC):
        part_chunk(0, j)
        own_chunk(0, j)
    for j in range(UNC, NC):
        part_chunk(0, j)
    for j in range(UNC, NC):
        own_chunk(0, j)
    back_weights(1)
    back_data(1, 1)
    for j in range(EARLY):
        send_part(1, j)
    back_data(1, 0)
    operator(1)
    for i in range(3):
        cs_to(i).wait_recv()
    first_step()

    for j in range(EARLY, NC):
        part_chunk(1, j)
    loop(NC, lambda j: own_chunk(1, j))
    last_step()

    for k in range(TX // 8):
        out_rows(k).wait()
    for j in range(NC):
        whole_fwd(j).wait_send()
        for i in range(2):
            whole_to(i, j).wait_send()
    for d in range(2):
        edge_to(d).wait_send()
        for u in range(2):
            tv_side(d, u).wait_send()
    for s in range(2):
        for d in range(2):
            w_side(s, d).wait_send()
        for k in range(2):
            for u in range(2):
                m_sib(s, k, u).wait_send()
        ct_sib(s).wait_send()
        ct_xp(s).wait_send()
        ct_fwd(s).wait_send()

        def drain(j, s=s):
            for d in range(2):
                halo(s, d, j).wait_send()
                z_own(s, d, j).wait_send()
                z_part(s, d, j).wait_send()
            x_sum(s, j).wait_send()

        loop(NC, drain)
    for i in range(3):
        cs_to(i).wait_send()


def per_device(volume, measured, blocks, ray_lists, counts):
    vmem, smem, anywhere = (
        pl.BlockSpec(memory_space=space) for space in (pltpu.VMEM, pltpu.SMEM, pl.ANY)
    )
    dma = pltpu.SemaphoreType.DMA
    return pl.pallas_call(
        kernel,
        out_shape=jax.ShapeDtypeStruct(volume.shape, F32),
        in_specs=[anywhere, anywhere, vmem, smem, smem],
        out_specs=anywhere,
        scratch_shapes=[
            pltpu.VMEM((2, NZ, 8, CY), F32),
            pltpu.VMEM((2, 3, NC, NZ, CH), F32),
            pltpu.VMEM((2, 2, 2, 2 * NA, DR, UC), F32),
            pltpu.VMEM((4, 2, 3, NZ, ROWS), F32),
            pltpu.VMEM((2, 2, NZ, ROWS), F32),
            pltpu.VMEM((4, 2, 8, 128), F32),
            pltpu.VMEM((2, 3 * NZ, 9 * NZ), BF),
            pltpu.VMEM((2, 3 * NZ, 6 * ROWS), BF),
            pltpu.VMEM((2, 3, NC, NZ, CH), F32),
            pltpu.VMEM((2, 3, NC, NZ, CH), F32),
            pltpu.VMEM((2, 2, NC, NZ, CH), F32),
            pltpu.VMEM((2, 2, NC, NZ, CH), F32),
            pltpu.VMEM((2, NC, NZ, CH), F32),
            pltpu.VMEM((2, NC, NZ, CH), F32),
            pltpu.VMEM((NC, NZ, CH), F32),
            pltpu.VMEM((2, 2, NZ, CY), F32),
            pltpu.VMEM((TX // UX, UNC, NZ, CH), F32),
            pltpu.VMEM((2, NZ, CY), F32),
            pltpu.VMEM((NZ, TX, CY), F32),
            dma((10 + TX // 8,)),
            dma((2, 2)), dma((2, 2)),
            dma((3, 2)), dma((3, 2)),
            dma((3,)), dma((3,)),
            dma((2, 2, 2)), dma((2, 2, 2)),
            dma((2, 2, NC)), dma((2, 2, NC)),
            dma((2, 2, NC)), dma((2, 2, NC)),
            dma((2, 2, NC)), dma((2, 2, NC)),
            dma((2, NC)), dma((2, NC)),
            dma((2, 2)), dma((2, 2)),
            dma((3, NC)), dma((3, NC)),
            dma((2,)), dma((2,)),
        ],
        compiler_params=pltpu.CompilerParams(
            collective_id=0, has_side_effects=True, vmem_limit_bytes=56 * 1024 * 1024
        ),
        name="sart_tv",
    )(volume, measured, blocks, ray_lists, counts)


def solution(mesh):
    return jax.shard_map(
        per_device,
        mesh=mesh,
        in_specs=(
            P(None, "tile", None),
            P(None, "angle", "tile", None),
            P(None, "angle", "tile", None, None),
            P(None, "angle", "tile"),
            P(None, "angle", "tile"),
        ),
        out_specs=P(None, "tile", None),
        check_vma=False,
    )
```

time: 191 us -> 173 us (0.906)
  Pallas kernels: 183 us -> 164 us
    pallas_call x1, Pallas kernels: 183 us -> 164 us  [per_device(): pl.pallas_call(kernel, out_shape=jax.ShapeDtypeStruct(volume.shape, F32),...]
where the time goes in v2:
time: 173 us; the launch traced here: 171 us
  Pallas kernels  164 us (95%)
  local copies, waits for them, and re-layouts  6.68 us (4%)
    pallas_call x1, Pallas kernels, per_device(): pl.pallas_call(kernel, out_shape=jax.ShapeDtypeStruct(volume.shape, F32),...  164 us
    unnamed x3, local copies, waits for them, and re-layouts  6.68 us

profile of v2, /device:TPU:1, one launch (start us, length us, event | category | flops | bytes accessed | tf_op | source)
XLA Modules:
  0.0 171.0 jit_solution(3995691558284213093)
XLA Ops:
  0.0 1.4 copy.6.ids
  1.4 1.4 copy.7.cnt
  2.7 164.3 %sart_tv.1 = f32[96,32,256]{2,1,0:T(8,128)} custom-call(f32[96,32,256]{2,1,0:T(8,128)} %vol.1, f32[2,8,16,8192]{3,2,1,0:T(8,128)} %meas.1, f32[2,8,3,16,96]{4,3,2,1,0:T(8,128)} %blk.1, s32[2,8,3]{2,1,0:T(8,128)} %copy.6.ids, s32[2,8,1]{2,1,0:T(8,128)} %copy.7.cnt), custom_call_target="tpu_custom_call" | custom-call | tf_op jit(solution)/shard_map/sart_tv/pallas_call | solution.py:504
  167.0 4.0 %copy.9 = f32[96,32,256]{2,1,0:T(8,128)} copy(f32[96,32,256]{2,1,0:T(8,128)} %sart_tv.1) | data formatting | bytes 6291456

commit v3 on v2

--- a/solution.py
+++ b/solution.py
@@ -18,6 +18,7 @@
 CH = 2 * UC // NC
 UNC = NC // 2
 EARLY = 2
+RELAY = (0, 1)
 RUN = 4
 NA, DR, SLOTS = 8, 16, 3
 ROWS = NA * DR
@@ -48,9 +49,9 @@
 
 
 def kernel(
-    vol, meas, blk, ids, cnt, out,
-    vq, xb, mb, ctb, csend, csb, gst, cst, po, pp, rz, rp, rsx, sp, xu, tvh, xall, edge, yt,
-    lsem, s_w, r_w, s_ct, r_ct, s_cs, r_cs, s_m, r_m, s_h, r_h, s_z, r_z, s_p, r_p, s_x, r_x, s_t, r_t, s_o, r_o, s_e, r_e,
+    vol, meas, blk, lists, out,
+    vq, xb, mb, ctb, csend, csb, gst, cst, po, pp, rz, rp, rsx, rly, sp, xu, tvh, xall, edge, yt,
+    lsem, s_w, r_w, s_ct, r_ct, s_cs, r_cs, s_m, r_m, s_h, r_h, s_z, r_z, s_p, r_p, s_x, r_x, s_y, r_y, s_v, s_t, r_t, s_o, r_o, s_e, r_e,
 ):
     t = lax.axis_index("tile")
     a = lax.axis_index("angle")
@@ -73,6 +74,11 @@
     def region(angle, u):
         up = upper(angle, u)
         return (1 - up) * angle + up * (4 + (angle + 2 * x_lo) % 4)
+
+    pair_t = t + 1 - 2 * (t % 2)
+    place = t % RUN
+    outer = (place == 0) | (place == RUN - 1)
+    inner = (place != 0) & (place != RUN - 1)
 
     b = (a + 2 * x_lo) % 4
     top, low = a // 3, 1 - (a + 3) // 4
@@ -146,6 +152,12 @@
     def x_sum(s, j):
         return remote(sp.at[s, j], rsx.at[s, j], s_x.at[s, j], r_x.at[s, j], xp)
 
+    def x_out(s, j):
+        return remote(sp.at[s, j], rly.at[s, j], s_y.at[s, j], r_y.at[s, j], (pair_t, a))
+
+    def x_relay(s, j):
+        return remote(rly.at[s, j], rsx.at[s, j], s_v.at[s, j], r_x.at[s, j], (pair_t, xp_a))
+
     def tv_side(d, u):
         src = x_ref(u, UX - 1) if d == 0 else x_ref(u, 0)
         tile, angle, slot = beside(d, u)
@@ -192,7 +204,7 @@
         for k in (1, 0):
             for u in range(2):
                 m_in(s, k, u).start()
-    peers = (sib, xp, diag) + tuple(side(d, u) for d in range(2) for u in range(2))
+    peers = (sib, xp, diag, (pair_t, xp_a)) + tuple(side(d, u) for d in range(2) for u in range(2))
     peers = peers + tuple(beside(d, u)[:2] for d in range(2) for u in range(2))
     barrier = pltpu.get_barrier_semaphore()
     for peer in peers:
@@ -205,7 +217,8 @@
             for n in range(NA):
                 block = jnp.zeros((DR, NZ), F32)
                 for k in range(SLOTS):
-                    live = (cnt[s, n, 0] > k) & (ids[s, n, k] - t == o - 1)
+                    entry = lists[s, n, k]
+                    live = (entry % 4 > k) & (entry // 4 - t == o - 1)
                     block = block + blk[s, n, k] * jnp.where(live, 1.0, 0.0).astype(F32)
                 rows.append(block)
             block = jnp.concatenate(rows, axis=0)
@@ -309,7 +322,24 @@
         for d in range(2):
             z_part(s, d, j).wait_recv()
         sp[s, j] = pp[s, 1, j] + rp[s, 0, j] + rp[s, 1, j]
-        x_sum(s, j).start()
+        if j not in RELAY:
+            x_sum(s, j).start()
+            return
+
+        @pl.when(inner)
+        def _():
+            x_sum(s, j).start()
+
+        @pl.when(outer)
+        def _():
+            x_out(s, j).start()
+
+    def relay(s):
+        @pl.when(inner)
+        def _():
+            for j in RELAY:
+                x_out(s, j).wait_recv()
+                x_relay(s, j).start()
 
     def scale(s):
         sums = csb[0, s] + csb[1, s] + csb[2, s] + csb[3, s]
@@ -439,18 +469,20 @@
     send_halo(0, 2)
     send_halo(0, 3)
     send_m(1)
+    weights_on(1)
     back_data(0, 0)
-    weights_on(1)
+    part_chunk(0, 0)
     operator(0)
-    for j in range(UNC):
-        part_chunk(0, j)
-        own_chunk(0, j)
-    for j in range(UNC, NC):
-        part_chunk(0, j)
+    part_chunk(0, 1)
+    own_chunk(0, 0)
+    part_chunk(0, 2)
+    own_chunk(0, 1)
+    part_chunk(0, 3)
     for j in range(UNC, NC):
         own_chunk(0, j)
     back_weights(1)
     back_data(1, 1)
+    relay(0)
     for j in range(EARLY):
         send_part(1, j)
     back_data(1, 0)
@@ -461,7 +493,10 @@
 
     for j in range(EARLY, NC):
         part_chunk(1, j)
-    loop(NC, lambda j: own_chunk(1, j))
+    for j in range(NC):
+        own_chunk(1, j)
+        if j == 1:
+            relay(1)
     last_step()
 
     for k in range(TX // 8):
@@ -489,9 +524,23 @@
                 halo(s, d, j).wait_send()
                 z_own(s, d, j).wait_send()
                 z_part(s, d, j).wait_send()
-            x_sum(s, j).wait_send()
 
         loop(NC, drain)
+        for j in range(NC):
+            if j not in RELAY:
+                x_sum(s, j).wait_send()
+
+        @pl.when(inner)
+        def _(s=s):
+            for j in RELAY:
+                x_sum(s, j).wait_send()
+                x_relay(s, j).wait_send()
+
+        @pl.when(outer)
+        def _(s=s):
+            for j in RELAY:
+                x_out(s, j).wait_send()
+
     for i in range(3):
         cs_to(i).wait_send()
 
@@ -500,11 +549,12 @@
     vmem, smem, anywhere = (
         pl.BlockSpec(memory_space=space) for space in (pltpu.VMEM, pltpu.SMEM, pl.ANY)
     )
+    lists = ray_lists * 4 + counts
     dma = pltpu.SemaphoreType.DMA
     return pl.pallas_call(
         kernel,
         out_shape=jax.ShapeDtypeStruct(volume.shape, F32),
-        in_specs=[anywhere, anywhere, vmem, smem, smem],
+        in_specs=[anywhere, anywhere, vmem, smem],
         out_specs=anywhere,
         scratch_shapes=[
             pltpu.VMEM((2, NZ, 8, CY), F32),
@@ -520,6 +570,7 @@
             pltpu.VMEM((2, 2, NC, NZ, CH), F32),
             pltpu.VMEM((2, 2, NC, NZ, CH), F32),
             pltpu.VMEM((2, NC, NZ, CH), F32),
+            pltpu.VMEM((2, max(RELAY) + 1, NZ, CH), F32),
             pltpu.VMEM((2, NC, NZ, CH), F32),
             pltpu.VMEM((NC, NZ, CH), F32),
             pltpu.VMEM((2, 2, NZ, CY), F32),
@@ -535,15 +586,16 @@
             dma((2, 2, NC)), dma((2, 2, NC)),
             dma((2, 2, NC)), dma((2, 2, NC)),
             dma((2, NC)), dma((2, NC)),
+            dma((2, NC)), dma((2, NC)), dma((2, NC)),
             dma((2, 2)), dma((2, 2)),
             dma((3, NC)), dma((3, NC)),
             dma((2,)), dma((2,)),
         ],
         compiler_params=pltpu.CompilerParams(
-            collective_id=0, has_side_effects=True, vmem_limit_bytes=56 * 1024 * 1024
+            collective_id=0, has_side_effects=True, vmem_limit_bytes=50 * 1024 * 1024
         ),
         name="sart_tv",
-    )(volume, measured, blocks, ray_lists, counts)
+    )(volume, measured, blocks, lists)
 
 
 def solution(mesh):

time: 173 us -> 159 us (0.919)
  Pallas kernels: 164 us -> 154 us
  local copies, waits for them, and re-layouts: 6.68 us -> 3.43 us
    pallas_call x1, Pallas kernels: 164 us -> 154 us  [per_device(): pl.pallas_call(kernel, out_shape=jax.ShapeDtypeStruct(volume.shape, F32),...]
    unnamed x3 -> x4, local copies, waits for them, and re-layouts: 6.68 us -> 3.43 us
where the time goes in v3:
time: 159 us; the launch traced here: 158 us
  Pallas kernels  154 us (97%)
  local copies, waits for them, and re-layouts  3.43 us (2%)
    pallas_call x1, Pallas kernels, per_device(): pl.pallas_call(kernel, out_shape=jax.ShapeDtypeStruct(volume.shape, F32),...  154 us
    unnamed x4, local copies, waits for them, and re-layouts  3.43 us

profile of v3, /device:TPU:1, one launch (start us, length us, event | category | flops | bytes accessed | tf_op | source)
XLA Modules:
  0.0 158.0 jit_solution(14950633181748803202)
XLA Ops:
  0.0 0.8 copy.6
  0.8 0.7 multiply_add_fusion.lists
  1.5 0.0 copy-start
  1.5 1.0 copy-done
  2.5 153.9 %sart_tv.1 = f32[96,32,256]{2,1,0:T(8,128)S(1)} custom-call(f32[96,32,256]{2,1,0:T(8,128)} %vol.1, f32[2,8,16,8192]{3,2,1,0:T(8,128)} %meas.1, f32[2,8,3,16,96]{4,3,2,1,0:T(8,128)S(1)} %copy-done, s32[2,8,3]{2,1,0:T(8,128)S(1)} %multiply_add_fusion.lists), custom_call_target="tpu_custom_call" | custom-call | tf_op jit(solution)/shard_map/sart_tv/pallas_call | solution.py:554
  156.4 1.7 %copy.8 = f32[96,32,256]{2,1,0:T(8,128)} copy(f32[96,32,256]{2,1,0:T(8,128)S(1)} %sart_tv.1) | data formatting | bytes 6291456
Async XLA Ops:
  1.5 1.0 copy-start

commit v4 on v3

--- a/solution.py
+++ b/solution.py
@@ -18,7 +18,7 @@
 CH = 2 * UC // NC
 UNC = NC // 2
 EARLY = 2
-RELAY = (0, 1)
+RELAY = ((0, 1), (0, 1, 2))
 RUN = 4
 NA, DR, SLOTS = 8, 16, 3
 ROWS = NA * DR
@@ -322,7 +322,7 @@
         for d in range(2):
             z_part(s, d, j).wait_recv()
         sp[s, j] = pp[s, 1, j] + rp[s, 0, j] + rp[s, 1, j]
-        if j not in RELAY:
+        if j not in RELAY[s]:
             x_sum(s, j).start()
             return
 
@@ -334,10 +334,16 @@
         def _():
             x_out(s, j).start()
 
+    def relay_one(s, j):
+        @pl.when(inner)
+        def _():
+            x_out(s, j).wait_recv()
+            x_relay(s, j).start()
+
     def relay(s):
         @pl.when(inner)
         def _():
-            for j in RELAY:
+            for j in RELAY[s]:
                 x_out(s, j).wait_recv()
                 x_relay(s, j).start()
 
@@ -495,8 +501,8 @@
         part_chunk(1, j)
     for j in range(NC):
         own_chunk(1, j)
-        if j == 1:
-            relay(1)
+        if j in RELAY[1]:
+            relay_one(1, j)
     last_step()
 
     for k in range(TX // 8):
@@ -527,18 +533,18 @@
 
         loop(NC, drain)
         for j in range(NC):
-            if j not in RELAY:
+            if j not in RELAY[s]:
                 x_sum(s, j).wait_send()
 
         @pl.when(inner)
         def _(s=s):
-            for j in RELAY:
+            for j in RELAY[s]:
                 x_sum(s, j).wait_send()
                 x_relay(s, j).wait_send()
 
         @pl.when(outer)
         def _(s=s):
-            for j in RELAY:
+            for j in RELAY[s]:
                 x_out(s, j).wait_send()
 
     for i in range(3):
@@ -570,7 +576,7 @@
             pltpu.VMEM((2, 2, NC, NZ, CH), F32),
             pltpu.VMEM((2, 2, NC, NZ, CH), F32),
             pltpu.VMEM((2, NC, NZ, CH), F32),
-            pltpu.VMEM((2, max(RELAY) + 1, NZ, CH), F32),
+            pltpu.VMEM((2, NC - 1, NZ, CH), F32),
             pltpu.VMEM((2, NC, NZ, CH), F32),
             pltpu.VMEM((NC, NZ, CH), F32),
             pltpu.VMEM((2, 2, NZ, CY), F32),

time: 159 us -> 156 us (0.981)
  Pallas kernels: 154 us -> 152 us
    pallas_call x1, Pallas kernels: 154 us -> 152 us  [per_device(): pl.pallas_call(kernel, out_shape=jax.ShapeDtypeStruct(volume.shape, F32),...]
where the time goes in v4:
time: 156 us
  Pallas kernels  152 us (97%)
  local copies, waits for them, and re-layouts  3.43 us (2%)
    pallas_call x1, Pallas kernels, per_device(): pl.pallas_call(kernel, out_shape=jax.ShapeDtypeStruct(volume.shape, F32),...  152 us
    unnamed x4, local copies, waits for them, and re-layouts  3.43 us

profile of v4, /device:TPU:1, one launch (start us, length us, event | category | flops | bytes accessed | tf_op | source)
XLA Modules:
  0.0 155.8 jit_solution(17146378515117002611)
XLA Ops:
  0.0 0.8 copy.6
  0.8 0.7 multiply_add_fusion.lists
  1.5 0.0 copy-start
  1.5 1.0 copy-done
  2.5 151.7 %sart_tv.1 = f32[96,32,256]{2,1,0:T(8,128)S(1)} custom-call(f32[96,32,256]{2,1,0:T(8,128)} %vol.1, f32[2,8,16,8192]{3,2,1,0:T(8,128)} %meas.1, f32[2,8,3,16,96]{4,3,2,1,0:T(8,128)S(1)} %copy-done, s32[2,8,3]{2,1,0:T(8,128)S(1)} %multiply_add_fusion.lists), custom_call_target="tpu_custom_call" | custom-call | tf_op jit(solution)/shard_map/sart_tv/pallas_call | solution.py:560
  154.2 1.7 %copy.8 = f32[96,32,256]{2,1,0:T(8,128)} copy(f32[96,32,256]{2,1,0:T(8,128)S(1)} %sart_tv.1) | data formatting | bytes 6291456
Async XLA Ops:
  1.5 1.0 copy-start
